TPU v7x, 32 devices: a whole 2x2x4 slice. The times are simulated.
32 devices in a mesh: sect: 2 (over core), tmpl: 16 (over z, y, x).
Axes of the slice: x: 2, y: 2, z: 4, core: 2. Of those that a mesh axis runs over, the one named last changes fastest.
Arguments:
- strain: bfloat16 [2, 1535], P('sect'), may hold values from -6 to 6
- filters: bfloat16 [2, 1024, 1024], P('sect', 'tmpl'), may hold values from -0.1875 to 0.1875
- synthesis: bfloat16 [2, 32768, 1024], P('sect', 'tmpl'), may hold values from -0.1875 to 0.1875
- correlation: float32 [16384, 2, 351], P('tmpl'), may hold values from -0.6 to 0.6
Outputs:
- snr: bfloat16 [32768, 512], P('tmpl', 'sect')
- residual: float32 [16384, 512], P('tmpl', 'sect')
All inputs are finite; a program needn't handle non-finite values.
Results may differ from a plain program's by a relative error of at most 0.0049.
Values may be sent and summed in bfloat16 or wider, within the bound.
A program may use at most 128 MiB of HBM per device.

v0:
```python
import numpy as np
import jax
import jax.numpy as jnp
from jax import lax
from jax.sharding import PartitionSpec as P

KMAX = 4
LANES = 128


def transforms(samples, share, sections, length):
    centre = (length - 1) // 2
    freqs = -(-(share + length - 1) // (2 * LANES)) * LANES
    omega = np.pi * (np.arange(freqs) + 0.5) / freqs
    times = np.arange(samples)
    angle = times[:, None] * omega[None, :]
    forward = np.concatenate([np.cos(angle), np.sin(angle)], axis=1)
    first = np.arange(sections)[:, None] * share
    near = (times[None] >= first - centre) & (times[None] < first + share + length - 1 - centre)
    forward = np.where(near[:, :, None], forward[None], 0.0)
    lags = (np.arange(length) - centre)[:, None] * omega[None, :]
    series = np.concatenate([np.cos(lags), np.sin(lags)], axis=1)
    back = angle.reshape(sections, share, freqs).transpose(0, 2, 1)
    inverse = np.concatenate([np.cos(back), -np.sin(back)], axis=1) / (2 * freqs)
    reach = times[None, :, None] - (first + np.arange(share)[None])[:, None, :]
    band = (reach >= -centre) & (reach < length - centre)
    return tuple(jnp.asarray(x, jnp.bfloat16) for x in (forward, series, inverse, band))


def dot(a, b):
    return jnp.dot(a, b, preferred_element_type=jnp.float32)


def filtered(signal, bank):
    taps = bank.shape[1]
    samples = signal.shape[0] - taps + 1
    rows = 2 * LANES
    padded = jnp.pad(signal, (0, -signal.shape[0] % LANES))
    width = padded.shape[0] + 1
    shifted = jnp.tile(padded, rows + 1)[: rows * width].reshape(rows, width)
    parts = [
        dot(bank[:, at : at + rows], shifted[:, at : at + samples])
        for at in range(0, taps, rows)
    ]
    return sum(parts[1:], parts[0])


def local(strain, filters, synthesis, correlation):
    sections = lax.axis_size("sect")
    section = lax.axis_index("sect")
    taps = filters.shape[2]
    samples = strain.shape[1] - taps + 1
    share = samples // sections
    length = correlation.shape[2]
    forward, series, inverse, band = transforms(samples, share, sections, length)
    freqs = series.shape[1] // 2
    forward, inverse, band = forward[section], inverse[section], band[section]
    basis = filtered(strain[0], filters[0]).astype(jnp.bfloat16)
    piece = lax.all_gather(basis, "tmpl", axis=0, tiled=True)
    held = jnp.repeat(piece[:, : samples // 2], 2, axis=1)
    piece = jnp.where(section == 0, held, piece)
    own = dot(synthesis[0], piece)
    other = lax.ppermute(own, "sect", [(0, 1), (1, 0)])
    snr = own + other
    a, b = correlation[:, 0, :], correlation[:, 1, :]
    weight = jnp.sum(a * a + b * b, axis=1)[:, None]
    at = dot(a.astype(jnp.bfloat16), series)
    bt = dot(b.astype(jnp.bfloat16), series)
    ac, as_, bc, bs = at[:, :freqs], at[:, freqs:], bt[:, :freqs], bt[:, freqs:]
    pr, pi, mr, mi = ac + bs, as_ - bc, ac - bs, as_ + bc
    pairs = snr.reshape(snr.shape[0] // 2, 2, samples)
    x, y = pairs[:, 0], pairs[:, 1]
    xt = dot(x.astype(jnp.bfloat16), forward)
    yt = dot(y.astype(jnp.bfloat16), forward)
    xc, xs, yc, ys = xt[:, :freqs], xt[:, freqs:], yt[:, :freqs], yt[:, freqs:]
    zpr, zpi, zmr, zmi = xc + ys, yc - xs, xc - ys, -xs - yc
    wpr, wpi = zpr * pr - zpi * pi, zpr * pi + zpi * pr
    wmr, wmi = zmr * mr - zmi * mi, zmr * mi + zmi * mr
    u = jnp.concatenate([wpr + wmr, wpi + wmi], axis=1).astype(jnp.bfloat16)
    v = jnp.concatenate([wpi - wmi, wmr - wpr], axis=1).astype(jnp.bfloat16)
    u = dot(u, inverse)
    v = dot(v, inverse)
    power = x * x + y * y
    high = power.astype(jnp.bfloat16)
    low = (power - high.astype(jnp.float32)).astype(jnp.bfloat16)
    energy = dot(high, band) + dot(low, band)
    centre = lax.dynamic_slice_in_dim(snr, section * share, share, 1)
    mid = centre.reshape(pairs.shape[0], 2, share)
    xm, ym = mid[:, 0], mid[:, 1]
    cross = xm * u + ym * v
    residual = (energy - 2.0 * cross + (xm * xm + ym * ym) * weight) / (2.0 * length)
    return centre.astype(jnp.bfloat16), residual


def solution(mesh):
    placed = (
        P("sect", None),
        P("sect", "tmpl", None),
        P("sect", "tmpl", None),
        P("tmpl", None, None),
    )
    return jax.shard_map(
        local,
        mesh=mesh,
        in_specs=placed,
        out_specs=(P("tmpl", "sect"), P("tmpl", "sect")),
        check_vma=False,
    )
```

profile of v0, /device:TPU:0, one launch (start us, length us, event | category | flops | bytes accessed | tf_op | source)
XLA Modules:
  0.0 152.5 jit_solution(8509964634593723309)
XLA Ops:
  7.2 0.0 all-gather.2.cloned.1.call-start
  7.2 0.7 reduce.1
  7.9 0.1 tile.4
  8.0 0.9 tile.10
  8.9 0.1 slice.97
  9.0 1.4 reshape.27
  10.4 0.2 fusion.64
  10.5 0.2 convolution_add_fusion.3
  10.7 0.2 convolution_add_fusion.2
  10.9 0.8 fusion.35
  11.7 0.0 all-gather.2.cloned.1.call-update
  11.7 58.1 %all-gather.2.cloned.1.call-done = bf16[1024,512]{1,0:T(8,128)(2,1)} async-done(((bf16[64,512]{1,0:T(8,128)(2,1)}), bf16[1024,512]{1,0:T(8,128)(2,1)}) %all-gather.2.cloned.1.call-update) | async-done | bytes 1048592 | tf_op jit(solution)/shard_map/all_gather | solution.py:59
  69.8 1.1 slice.105
  70.9 0.2 copy.11
  71.1 0.5 broadcast_in_dim.4
  71.7 0.6 reshape.28
  72.3 1.3 copy.12
  73.6 7.0 %fusion.2 = f32[2048,512]{0,1:T(8,128)} fusion(bf16[1,2048,1024]{2,1,0:T(8,128)(2,1)} %param.10, bf16[1024,512]{1,0:T(8,128)(2,1)} %copy.12, bf16[1024,512]{1,0:T(8,128)(2,1)} %all-gather.2.cloned.1.call-done, pred[]{:T(512)S(6)} %eq.3), kind=kOutput, calls=%fused_computation.2 | convolution fusion | flops 2148007936 | bytes 10485761 | tf_op jit(solution)/shard_map/dot_general | solution.py:31
  80.7 2.2 %fusion.84 = (f32[1024,1,351]{0,1,2:T(1,128)S(1)}, f32[1024,1,351]{0,1,2:T(1,128)S(1)}) fusion(f32[1024,2,351]{0,1,2:T(2,128)S(1)} %copy-done.7), kind=kLoop, calls=%fused_computation.98 | loop fusion | bytes 5750784 | tf_op jit(solution)/shard_map/slice | solution.py:65
  82.9 0.7 add_reduce_fusion
  83.6 0.4 copy-done.8
  83.9 1.0 convolution_bitcast_fusion.1
  85.0 2.7 %convolution_bitcast_fusion = f32[1024,768]{0,1:T(8,128)} fusion(bf16[351,768]{1,0:T(8,128)(2,1)S(1)} %copy-done.8, f32[1024,1,351]{0,1,2:T(1,128)S(1)} %get-tuple-element.22), kind=kOutput, calls=%fused_computation.5 | convolution fusion | flops 552075264 | bytes 5122560 | tf_op jit(solution)/shard_map/dot_general | solution.py:31
  87.7 0.5 collective-permute-done
  88.2 6.5 %add.70 = f32[2048,512]{0,1:T(8,128)} add(f32[2048,512]{0,1:T(8,128)} %fusion.2, f32[2048,512]{0,1:T(8,128)} %collective-permute-done) | non-fusion elementwise | flops 1048576 | bytes 12582912 | tf_op jit(solution)/shard_map/add | solution.py:64
  94.7 5.4 %copy.13 = f32[2048,512]{1,0:T(8,128)} copy(f32[2048,512]{0,1:T(8,128)} %add.70) | data formatting | bytes 8388608 | tf_op jit(solution)/shard_map/add | solution.py:64
  100.0 5.9 %reshape.29 = f32[1024,2,512]{2,1,0:T(2,128)} reshape(f32[2048,512]{1,0:T(8,128)} %copy.13) | data formatting | bytes 8388608 | tf_op jit(solution)/shard_map/reshape | solution.py:71
  105.9 8.5 %subtract_convert_fusion = (bf16[1024,1,512]{2,1,0:T(2,128)(2,1)}, bf16[1024,1,512]{2,1,0:T(2,128)(2,1)}) fusion(f32[1024,2,512]{2,1,0:T(2,128)} %reshape.29), kind=kLoop, calls=%fused_computation.3 | loop fusion | flops 4194304 | bytes 6291456 | tf_op jit(solution)/shard_map/convert_element_type | solution.py:85
  114.4 4.2 %fusion.83 = (bf16[1024,1,512]{2,1,0:T(2,128)(2,1)}, bf16[1024,1,512]{2,1,0:T(2,128)(2,1)}) fusion(f32[1024,2,512]{2,1,0:T(2,128)S(1)} %copy-done), kind=kLoop, calls=%fused_computation.97 | loop fusion | bytes 4194304 | tf_op jit(solution)/shard_map/slice | solution.py:72
  118.7 2.0 %fusion.82 = (bf16[2048,256]{0,1:T(8,128)(2,1)}, f32[2048,256]{0,1:T(8,128)}) fusion(f32[2048,512]{0,1:T(8,128)S(1)} %copy-done.1, s32[]{:T(128)S(6)} %select_n.18), kind=kLoop, calls=%fused_computation.96 | loop fusion | flops 524288 | bytes 5242884 | tf_op jit(solution)/shard_map/convert_element_type | solution.py:92
  120.7 2.3 %copy.19 = bf16[2048,256]{1,0:T(8,128)(2,1)} copy(bf16[2048,256]{0,1:T(8,128)(2,1)} %get-tuple-element.14) | data formatting | bytes 2097152
  122.9 2.9 %copy.14 = f32[2048,256]{1,0:T(8,128)} copy(f32[2048,256]{0,1:T(8,128)} %get-tuple-element.15) | data formatting | bytes 4194304 | tf_op jit(solution)/shard_map/dynamic_slice | solution.py:87
  125.8 3.5 %reshape.30 = f32[1024,2,256]{2,1,0:T(2,128)} reshape(f32[2048,256]{1,0:T(8,128)} %copy.14) | data formatting | bytes 4194304 | tf_op jit(solution)/shard_map/reshape | solution.py:88
  129.3 4.2 %fusion.85 = (f32[1024,1,256]{2,1,0:T(1,128)S(1)}, f32[1024,1,256]{2,1,0:T(1,128)S(1)}) fusion(f32[1024,2,256]{2,1,0:T(2,128)} %reshape.30), kind=kLoop, calls=%fused_computation.99 | loop fusion | bytes 4194304 | tf_op jit(solution)/shard_map/slice | solution.py:89
  133.5 1.1 fusion.39
  134.6 0.5 copy-done.4
  135.1 1.0 fusion.36
  136.2 0.5 copy-done.3
  136.7 0.1 copy-done.10
  136.8 0.4 fusion.44
  137.2 0.7 copy-done.6
  137.9 0.4 convolution_add_fusion
  138.4 1.4 copy-done.2
  139.8 2.0 %subtract_convert_fusion.1 = (bf16[1024,384]{0,1:T(8,128)(2,1)S(1)}, f32[1024,384]{0,1:T(8,128)S(1)}, f32[1024,384]{0,1:T(8,128)S(1)}, bf16[1024,384]{0,1:T(8,12...) fusion(f32[1024,768]{0,1:T(8,128)S(1)} %copy-done.2, f32[1024,768]{0,1:T(8,128)S(1)} %convolution_bitcast_fusion.1, ...), kind=kLoop, calls=%fused_computation.15 | loop fusion | flops 9830400 | bytes 20447232 | tf_op jit(solution)/shard_map/convert.1
  141.9 0.8 add_convert_fusion
  142.7 0.3 copy-done.12
  143.0 0.6 fusion.31
  143.6 2.0 %fusion.28 = f32[1024,256]{1,0:T(8,128)} fusion(f32[1024,256]{1,0:T(8,128)S(1)} %convolution_add_fusion, f32[1024,256]{1,0:T(8,128)S(1)} %fusion.31, bf16[1024,384]{0,1:T(8,128)(2,1)S(1)} %get-tuple-element.9, bf16[1024,384]{0,1:T(8,128)(2,1)S(1)} %get-tuple-element.16, f32[1024,1,256]{2,1,0:T(1,128)S(1)} %get-tuple-element.23, ...), kind=kOutput, calls=%fused_computation.37 | convolution fusion | flops 408420352 | bytes 7213060 | tf_op jit(solution)/shard_map/dot_general | solution.py:31
  (21 shorter events, 0.1 us)
Async XLA Ops:
  7.2 62.7 %all-gather.2.cloned.1.call-start = ((), (), s32[]{:S(2)}) async-start(), calls=%async_computation | async-start | bytes 1114112 | tf_op jit(solution)/shard_map/all_gather | solution.py:59
  8.9 1.5 copy-start.11
  73.6 7.0 %copy-start.7 = (f32[1024,2,351]{0,1,2:T(2,128)S(1)}, f32[1024,2,351]{0,1,2:T(2,128)}, u32[]{:S(2)}) copy-start(f32[1024,2,351]{0,1,2:T(2,128)} %param.11) | copy-start | bytes 8626180
  80.7 7.5 %collective-permute-start = (f32[2048,512]{0,1:T(8,128)}, f32[2048,512]{0,1:T(8,128)}, u32[]{:S(2)}, u32[]{:S(2)}) collective-permute-start(f32[2048,512]{0,1:T(8,128)} %fusion.2), channel_id=1, source_target_pairs={{0,16},{16,0},{1,17},{17,1},{2,18},{18,2},{3,19},{19,3},{4,20},{20... | collective-permute-start | bytes 12582920 | tf_op jit(solution)/shard_map/ppermute | solution.py:63
  82.9 1.1 copy-start.8
  105.9 8.5 %copy-start = (f32[1024,2,512]{2,1,0:T(2,128)S(1)}, f32[1024,2,512]{2,1,0:T(2,128)}, u32[]{:S(2)}) copy-start(f32[1024,2,512]{2,1,0:T(2,128)} %reshape.29) | copy-start | bytes 12582916
  114.4 4.2 %copy-start.1 = (f32[2048,512]{0,1:T(8,128)S(1)}, f32[2048,512]{0,1:T(8,128)}, u32[]{:S(2)}) copy-start(f32[2048,512]{0,1:T(8,128)} %add.70) | copy-start | bytes 12582916
  129.3 4.2 %copy-start.5 = (bf16[1024,1,512]{2,1,0:T(2,128)(2,1)S(1)}, bf16[1024,1,512]{2,1,0:T(2,128)(2,1)}, u32[]{:S(2)}) copy-start(bf16[1024,1,512]{2,1,0:T(2,128)(2,1)} %get-tuple-element.19) | copy-start | bytes 3145732
  129.3 4.2 %copy-start.9 = (bf16[2,512,768]{2,1,0:T(8,128)(2,1)S(1)}, bf16[2,512,768]{2,1,0:T(8,128)(2,1)}, u32[]{:S(2)}) copy-start(bf16[2,512,768]{2,1,0:T(8,128)(2,1)} %constant.31.clone) | copy-start | bytes 4718596
  133.5 1.6 %copy-start.4 = (bf16[1024,1,512]{2,1,0:T(2,128)(2,1)S(1)}, bf16[1024,1,512]{2,1,0:T(2,128)(2,1)}, u32[]{:S(2)}) copy-start(bf16[1024,1,512]{2,1,0:T(2,128)(2,1)} %get-tuple-element.20) | copy-start | bytes 3145732
  135.1 1.6 %copy-start.3 = (bf16[1024,1,512]{2,1,0:T(2,128)(2,1)S(1)}, bf16[1024,1,512]{2,1,0:T(2,128)(2,1)}, u32[]{:S(2)}) copy-start(bf16[1024,1,512]{2,1,0:T(2,128)(2,1)} %get-tuple-element.13) | copy-start | bytes 3145732
  135.1 1.7 %copy-start.10 = (bf16[2,512,256]{2,1,0:T(8,128)(2,1)S(1)}, bf16[2,512,256]{2,1,0:T(8,128)(2,1)}, u32[]{:S(2)}) copy-start(bf16[2,512,256]{2,1,0:T(8,128)(2,1)} %constant.34.clone) | copy-start | bytes 1572868
  136.2 1.8 %copy-start.6 = (bf16[1024,1,512]{2,1,0:T(2,128)(2,1)S(1)}, bf16[1024,1,512]{2,1,0:T(2,128)(2,1)}, u32[]{:S(2)}) copy-start(bf16[1024,1,512]{2,1,0:T(2,128)(2,1)} %get-tuple-element.12) | copy-start | bytes 3145732
  137.9 1.9 %copy-start.2 = (f32[1024,768]{0,1:T(8,128)S(1)}, f32[1024,768]{0,1:T(8,128)}, u32[]{:S(2)}) copy-start(f32[1024,768]{0,1:T(8,128)} %convolution_bitcast_fusion) | copy-start | bytes 9437188
  141.9 1.1 copy-start.12
Sparse Core Ops, SparseCore 0:
  11.8 57.9 all-gather.1
where the time goes:
time: 153 us; the launch traced here: 152 us
  waiting for transfers between devices  58.6 us (38%)
  local copies, waits for them, and re-layouts  40.6 us (27%)
  other arithmetic  21.3 us (14%)
  matrix products  17.6 us (12%)
  between operations  14.3 us (9%)
    all_gather x1, waiting for transfers between devices, local(): piece = lax.all_gather(basis, 'tmpl', axis=0, tiled=True)  58.1 us
    dot_general x13, matrix products, dot(): return jnp.dot(a, b, preferred_element_type=jnp.float32)  17.6 us
    convert_element_type x1, other arithmetic, local(): low = (power - high.astype(jnp.float32)).astype(jnp.bfloat16)  8.52 us
    add x1, other arithmetic, local(): snr = own + other  6.51 us
    unnamed x27, local copies, waits for them, and re-layouts  6.22 us
    reshape x1, local copies, waits for them, and re-layouts, local(): pairs = snr.reshape(snr.shape[0] // 2, 2, samples)  5.87 us
    add x1, local copies, waits for them, and re-layouts, local(): snr = own + other  5.36 us
    slice x1, local copies, waits for them, and re-layouts, local(): x, y = (pairs[:, 0], pairs[:, 1])  4.23 us
  transfers between devices with their start and end apart: 2, of which 2 were waited for; matrix products, arithmetic and copies ran while one was open for 4% of the time, Pallas kernels for 0%

commit v1 on v0

v1 whole, which is shorter than its diff:
```python
import functools

import numpy as np
import jax
import jax.numpy as jnp
from jax import lax
from jax.experimental import pallas as pl
from jax.experimental.pallas import tpu as pltpu
from jax.sharding import PartitionSpec as P

LANES = 128
TAP_GROUP = 256
CHUNK = 256
MESH = pl.DeviceIdType.MESH


def transforms(samples, share, sections, length):
    centre = (length - 1) // 2
    freqs = -(-(share + length - 1) // (2 * LANES)) * LANES
    depth = -(-length // LANES) * LANES
    omega = np.pi * (np.arange(freqs) + 0.5) / freqs
    times = np.arange(samples)
    angle = times[:, None] * omega[None, :]
    forward = np.concatenate([np.cos(angle), np.sin(angle)], axis=1)
    first = np.arange(sections)[:, None] * share
    near = (times[None] >= first - centre) & (times[None] < first + share + length - 1 - centre)
    forward = np.where(near[:, :, None], forward[None], 0.0)
    lags = (np.arange(depth) - centre)[:, None] * omega[None, :]
    series = np.concatenate([np.cos(lags), np.sin(lags)], axis=1)
    series = np.where(np.arange(depth)[:, None] < length, series, 0.0)
    back = angle.reshape(sections, share, freqs).transpose(0, 2, 1)
    inverse = np.concatenate([np.cos(back), -np.sin(back)], axis=1) / (2 * freqs)
    reach = times[None, :, None] - (first + np.arange(share)[None])[:, None, :]
    band = (reach >= -centre) & (reach < length - centre)
    return tuple(np.asarray(x, jnp.bfloat16) for x in (forward, series, inverse, band))


def dot(a, b):
    return jnp.dot(a, b, preferred_element_type=jnp.float32)


def kernel(
    length,
    strain_ref, filters_ref, synthesis_hbm, lags_hbm, weight_ref,
    forward_hbm, series_hbm, inverse_hbm, band_hbm,
    snr_hbm, residual_hbm,
    synthesis, lags, forward, series, inverse, band,
    gathered, own, theirs, spectra, full, turned, snr_out, residual_out,
    in_sems, out_sems, gather_send, gather_recv, swap_send, swap_recv,
):
    n = lax.axis_size("tmpl")
    me = lax.axis_index("tmpl")
    section = lax.axis_index("sect")
    block, samples = filters_ref.shape[0], gathered.shape[1]
    taps = filters_ref.shape[1]
    share = residual_out.shape[1]
    rows = synthesis.shape[0]
    chunks = rows // CHUNK
    half = CHUNK // 2
    tiles = spectra.shape[1]

    loads = [
        pltpu.make_async_copy(src, dst, in_sems.at[i])
        for i, (src, dst) in enumerate([
            (lags_hbm, lags),
            (series_hbm, series),
            (synthesis_hbm.at[0], synthesis),
            (forward_hbm.at[section], forward),
            (inverse_hbm.at[section], inverse),
            (band_hbm.at[section], band),
        ])
    ]
    for load in loads:
        load.start()

    barrier = pltpu.get_barrier_semaphore()

    def greet(step, carry):
        pl.semaphore_signal(
            barrier, inc=1, device_id={"tmpl": lax.rem(me + step, n)}, device_id_type=MESH
        )
        return carry

    lax.fori_loop(1, n, greet, 0)
    pl.semaphore_signal(barrier, inc=1, device_id={"sect": 1 - section}, device_id_type=MESH)

    wide = jnp.broadcast_to(strain_ref[...], (TAP_GROUP, strain_ref.shape[1]))
    width = wide.shape[1]
    hankel = pltpu.roll(wide, width - (TAP_GROUP - 1), 1, stride=1, stride_axis=0)
    hankel = hankel.astype(jnp.bfloat16)
    down = lax.broadcasted_iota(jnp.int32, (TAP_GROUP, TAP_GROUP), 0)
    across = lax.broadcasted_iota(jnp.int32, (TAP_GROUP, TAP_GROUP), 1)
    flip = jnp.where(down + across == TAP_GROUP - 1, 1.0, 0.0).astype(jnp.bfloat16)
    basis = jnp.zeros((block, samples), jnp.float32)
    for at in range(0, taps, TAP_GROUP):
        bank = dot(filters_ref[:, at : at + TAP_GROUP], flip).astype(jnp.bfloat16)
        basis = basis + dot(bank, hankel[:, at : at + samples])
    source = lax.broadcasted_iota(jnp.int32, (samples, samples), 0)
    target = lax.broadcasted_iota(jnp.int32, (samples, samples), 1)
    target = jnp.where(section == 0, target >> 1, target)
    hold = jnp.where(source == target, 1.0, 0.0).astype(jnp.bfloat16)
    mine = gathered.at[pl.ds(pl.multiple_of(me * block, block), block)]
    mine[...] = dot(basis.astype(jnp.bfloat16), hold).astype(jnp.bfloat16)

    pl.semaphore_wait(barrier, n)

    def push(step):
        return pltpu.make_async_remote_copy(
            src_ref=mine,
            dst_ref=mine,
            send_sem=gather_send.at[step],
            recv_sem=gather_recv.at[step],
            device_id={"tmpl": lax.rem(me + step, n)},
            device_id_type=MESH,
        )

    def start_push(step, carry):
        push(step).start()
        return carry

    def wait_push(step, carry):
        push(step).wait()
        return carry

    lax.fori_loop(1, n, start_push, 0)

    loads[0].wait()
    loads[1].wait()

    def analyse(c, carry):
        at = pl.ds(pl.multiple_of(c * half, half), half)
        real = dot(lags[0, at, :], series[...])
        imag = dot(lags[1, at, :], series[...])
        for i in range(tiles):
            cos = slice(i * LANES, (i + 1) * LANES)
            sin = slice((tiles + i) * LANES, (tiles + i + 1) * LANES)
            ac, as_, bc, bs = real[:, cos], real[:, sin], imag[:, cos], imag[:, sin]
            spectra[0, i, at, :] = ac + bs
            spectra[1, i, at, :] = as_ - bc
            spectra[2, i, at, :] = ac - bs
            spectra[3, i, at, :] = as_ + bc
        return carry

    lax.fori_loop(0, chunks, analyse, 0)
    for load in loads[2:]:
        load.wait()
    lax.fori_loop(1, n, wait_push, 0)

    def swap(c):
        at = pl.ds(pl.multiple_of(c * CHUNK, CHUNK), CHUNK)
        return pltpu.make_async_remote_copy(
            src_ref=own.at[at],
            dst_ref=theirs.at[at],
            send_sem=swap_send.at[c],
            recv_sem=swap_recv.at[c],
            device_id={"sect": 1 - section},
            device_id_type=MESH,
        )

    def reconstruct(c, carry):
        at = pl.ds(pl.multiple_of(c * CHUNK, CHUNK), CHUNK)
        value = dot(synthesis[at, :], gathered[...])
        own[at, :] = value.astype(jnp.bfloat16)
        swap(c).start()
        for i in range(samples // LANES):
            full[i, at, :] = value[:, i * LANES : (i + 1) * LANES]
        return carry

    lax.fori_loop(0, chunks, reconstruct, 0)

    def emit(c):
        at = pl.ds(pl.multiple_of(c * CHUNK, CHUNK), CHUNK)
        to = pl.ds(pl.multiple_of(c * half, half), half)
        return (
            pltpu.make_async_copy(snr_out.at[at], snr_hbm.at[at], out_sems.at[0, c]),
            pltpu.make_async_copy(residual_out.at[to], residual_hbm.at[to], out_sems.at[1, c]),
        )

    def resolve(c, carry):
        start = pl.multiple_of(c * CHUNK, CHUNK)
        at = pl.ds(start, CHUNK)
        to = pl.ds(pl.multiple_of(c * half, half), half)
        even = pl.ds(start, half, stride=2)
        odd = pl.ds(start + 1, half, stride=2)
        swap(c).wait()
        parts = []
        for i in range(samples // LANES):
            part = full[i, at, :] + theirs[at, i * LANES : (i + 1) * LANES].astype(jnp.float32)
            full[i, at, :] = part
            parts.append(part.astype(jnp.bfloat16))
        spectrum = dot(jnp.concatenate(parts, axis=1), forward[...])
        for i in range(2 * tiles):
            turned[i] = spectrum[:, i * LANES : (i + 1) * LANES]
        evens, odds = pl.ds(0, half, stride=2), pl.ds(1, half, stride=2)
        ur, ui, vr, vi = [], [], [], []
        for i in range(tiles):
            xc, yc = turned[i, evens, :], turned[i, odds, :]
            xs, ys = turned[tiles + i, evens, :], turned[tiles + i, odds, :]
            pr, pi = spectra[0, i, to, :], spectra[1, i, to, :]
            mr, mi = spectra[2, i, to, :], spectra[3, i, to, :]
            zpr, zpi, zmr, zmi = xc + ys, yc - xs, xc - ys, -xs - yc
            wpr, wpi = zpr * pr - zpi * pi, zpr * pi + zpi * pr
            wmr, wmi = zmr * mr - zmi * mi, zmr * mi + zmi * mr
            ur.append((wpr + wmr).astype(jnp.bfloat16))
            ui.append((wpi + wmi).astype(jnp.bfloat16))
            vr.append((wpi - wmi).astype(jnp.bfloat16))
            vi.append((wmr - wpr).astype(jnp.bfloat16))
        u = dot(jnp.concatenate(ur + ui, axis=1), inverse[...])
        v = dot(jnp.concatenate(vr + vi, axis=1), inverse[...])
        high, low = [], []
        for i in range(samples // LANES):
            x, y = full[i, even, :], full[i, odd, :]
            power = x * x + y * y
            top = power.astype(jnp.bfloat16)
            high.append(top)
            low.append((power - top.astype(jnp.float32)).astype(jnp.bfloat16))
        energy = dot(jnp.concatenate(high, axis=1), band[...])
        energy = energy + dot(jnp.concatenate(low, axis=1), band[...])
        weight = weight_ref[to, :]
        for i in range(share // LANES):
            columns = slice(i * LANES, (i + 1) * LANES)
            tile = section * (share // LANES) + i
            snr_out[at, columns] = full[tile, at, :].astype(jnp.bfloat16)
            x, y = full[tile, even, :], full[tile, odd, :]
            cross = x * u[:, columns] + y * v[:, columns]
            value = energy[:, columns] - 2.0 * cross + (x * x + y * y) * weight
            residual_out[to, columns] = value / (2.0 * length)
        for copy in emit(c):
            copy.start()
        return carry

    lax.fori_loop(0, chunks, resolve, 0)

    def finish(c, carry):
        for copy in emit(c):
            copy.wait()
        return carry

    lax.fori_loop(0, chunks, finish, 0)


def local(strain, filters, synthesis, correlation):
    sections = lax.axis_size("sect")
    n = lax.axis_size("tmpl")
    block, taps = filters.shape[1:]
    samples = strain.shape[1] - taps + 1
    share = samples // sections
    rows = synthesis.shape[1]
    groups, _, length = correlation.shape
    forward, series, inverse, band = transforms(samples, share, sections, length)
    depth, spectrum = series.shape
    tiles = spectrum // (2 * LANES)
    chunks = rows // CHUNK
    signal = jnp.pad(strain, ((0, 0), (0, -strain.shape[1] % LANES))).astype(jnp.float32)
    lags = jnp.pad(correlation, ((0, 0), (0, 0), (0, depth - length))).transpose(1, 0, 2)
    weight = jnp.sum(correlation * correlation, axis=(1, 2))[:, None]
    vmem = pl.BlockSpec(memory_space=pltpu.VMEM)
    hbm = pl.BlockSpec(memory_space=pl.ANY)
    return pl.pallas_call(
        functools.partial(kernel, length),
        out_shape=(
            jax.ShapeDtypeStruct((rows, share), jnp.bfloat16),
            jax.ShapeDtypeStruct((groups, share), jnp.float32),
        ),
        in_specs=[vmem, vmem, hbm, hbm, vmem, hbm, hbm, hbm, hbm],
        out_specs=(hbm, hbm),
        scratch_shapes=[
            pltpu.VMEM((rows, n * block), jnp.bfloat16),
            pltpu.VMEM((2, groups, depth), jnp.bfloat16),
            pltpu.VMEM(forward.shape[1:], jnp.bfloat16),
            pltpu.VMEM(series.shape, jnp.bfloat16),
            pltpu.VMEM(inverse.shape[1:], jnp.bfloat16),
            pltpu.VMEM(band.shape[1:], jnp.bfloat16),
            pltpu.VMEM((n * block, samples), jnp.bfloat16),
            pltpu.VMEM((rows, samples), jnp.bfloat16),
            pltpu.VMEM((rows, samples), jnp.bfloat16),
            pltpu.VMEM((4, tiles, groups, LANES), jnp.float32),
            pltpu.VMEM((samples // LANES, rows, LANES), jnp.float32),
            pltpu.VMEM((2 * tiles, CHUNK, LANES), jnp.float32),
            pltpu.VMEM((rows, share), jnp.bfloat16),
            pltpu.VMEM((groups, share), jnp.float32),
            pltpu.SemaphoreType.DMA((6,)),
            pltpu.SemaphoreType.DMA((2, chunks)),
            pltpu.SemaphoreType.DMA((n,)),
            pltpu.SemaphoreType.DMA((n,)),
            pltpu.SemaphoreType.DMA((chunks,)),
            pltpu.SemaphoreType.DMA((chunks,)),
        ],
        compiler_params=pltpu.CompilerParams(
            collective_id=0, has_side_effects=True, vmem_limit_bytes=56 * 2**20
        ),
    )(
        signal, filters[0], synthesis, lags.astype(jnp.bfloat16), weight,
        forward, series, inverse, band,
    )


def solution(mesh):
    placed = (
        P("sect", None),
        P("sect", "tmpl", None),
        P("sect", "tmpl", None),
        P("tmpl", None, None),
    )
    return jax.shard_map(
        local,
        mesh=mesh,
        in_specs=placed,
        out_specs=(P("tmpl", "sect"), P("tmpl", "sect")),
        check_vma=False,
    )
```

time: 153 us -> 55.5 us (0.36)
  the two profiles are of different devices: /device:TPU:0 before, /device:TPU:15 now
where the time goes in v1:
time: 55.5 us; the launch traced here: 55.3 us
  Pallas kernels  41.1 us (74%)
  local copies, waits for them, and re-layouts  7.64 us (14%)
  other arithmetic  5.9 us (11%)
  between operations  0.66 us (1%)
    pallas_call x1, Pallas kernels, local(): pl.pallas_call(functools.partial(kernel, length), out_shape=(jax.ShapeDty...  41.1 us
    reduce_sum x1, other arithmetic, local(): weight = jnp.sum(correlation * correlation, axis=(1, 2))[:, None]  4.61 us
    unnamed x4, local copies, waits for them, and re-layouts  3.32 us
    another operation x1, local copies, waits for them, and re-layouts  1.96 us
    convert_element_type x1, local copies, waits for them, and re-layouts, local(): lags.astype(jnp.bfloat16)  1.33 us
    convert_element_type x1, other arithmetic, local(): jnp.pad(strain, ((0, 0), (0, -strain.shape[1] % LANES))).astype(jnp.float32)  1.29 us

profile of v1, /device:TPU:15, one launch (start us, length us, event | category | flops | bytes accessed | tf_op | source)
XLA Modules:
  0.0 55.3 jit_solution(680476714490002278)
XLA Ops:
  0.6 1.3 %pad_convert_fusion.strain_ref = f32[1,1536]{1,0:T(1,128)} fusion(bf16[1,1535]{1,0:T(2,128)(2,1)} %param.8), kind=kLoop, calls=%fused_computation.2 | loop fusion | flops 1536 | bytes 9214 | tf_op jit(solution)/shard_map/convert_element_type | solution.py:254
  1.9 4.6 %multiply_reduce_fusion = (f32[1024]{0:T(1024)S(1)}, bf16[1024,2,351]{0,1,2:T(2,128)(2,1)S(1)}) fusion(f32[1024,2,351]{0,1,2:T(2,128)} %param.11), kind=kLoop, calls=%fused_computation | loop fusion | flops 2155520 | bytes 4317184 | tf_op jit(solution)/shard_map/reduce_sum | solution.py:256
  6.5 1.0 %copy.14.weight_ref = f32[1024,1]{1,0:T(8,128)} copy(f32[1024,1]{0,1:T(1,128)S(1)} %bitcast.5) | data formatting | bytes 8192 | tf_op jit(solution)/shard_map/broadcast_in_dim | solution.py:256
  7.6 2.0 %copy.13 = bf16[1024,2,351]{2,0,1:T(8,128)(2,1)S(1)} copy(bf16[1024,2,351]{0,1,2:T(2,128)(2,1)S(1)} %get-tuple-element.3) | data formatting | bytes 2875392 | tf_op jit(solution)/shard_map/convert
  9.5 1.3 %pad_bitcast_fusion.lags_hbm = bf16[2,1024,384]{2,1,0:T(8,128)(2,1)} fusion(bf16[1024,2,351]{2,0,1:T(8,128)(2,1)S(1)} %copy.13), kind=kLoop, calls=%fused_computation.1 | loop fusion | bytes 3010560 | tf_op jit(solution)/shard_map/convert_element_type | solution.py:293
  10.9 41.1 %shard_map.95 = (bf16[2048,256]{1,0:T(8,128)(2,1)}, f32[1024,256]{1,0:T(8,128)}) custom-call(f32[1,1536]{1,0:T(1,128)} %pad_convert_fusion.strain_ref, bf16[64,1024]{1,0:T(8,128)(2,1)} %bitcast.4, bf16[1,2048,1024]{2,1,0:T(8,128)(2,1)} %synthesis_hbm.1, bf16[2,1024,384]{2,1,0:T(8,128)(2,1)} %pad_bitcast_fusion.lags_hbm, f32[1024,1]{1,0:T(8,128)} %copy.14.weight_ref, ...), custom_call_target="tpu_custom_call" | custom-call | tf_op jit(solution)/shard_map/pallas_call | solution.py:259
  52.0 0.0 copy-start
  52.0 2.4 %copy.17 = bf16[2048,256]{1,0:T(8,128)(2,1)} copy(bf16[2048,256]{1,0:T(8,128)(2,1)} %get-tuple-element.6) | data formatting | bytes 2097152
  54.3 0.0 copy-done
  54.3 1.0 %copy.18 = f32[1024,256]{1,0:T(8,128)} copy(f32[1024,256]{1,0:T(8,128)S(1)} %copy-done) | data formatting | bytes 2097152
Async XLA Ops:
  52.0 2.4 %copy-start = (f32[1024,256]{1,0:T(8,128)S(1)}, f32[1024,256]{1,0:T(8,128)}, u32[]{:S(2)}) copy-start(f32[1024,256]{1,0:T(8,128)} %get-tuple-element.7) | copy-start | bytes 3145732

commit v2 on v1

--- a/solution.py
+++ b/solution.py
@@ -39,14 +39,18 @@
     return jnp.dot(a, b, preferred_element_type=jnp.float32)
 
 
+def dot_rows(a, b):
+    return lax.dot_general(a, b, (((0,), (0,)), ((), ())), preferred_element_type=jnp.float32)
+
+
 def kernel(
-    length,
-    strain_ref, filters_ref, synthesis_hbm, lags_hbm, weight_ref,
+    length, grid,
+    strain_ref, filters_ref, synthesis_hbm, lags_hbm,
     forward_hbm, series_hbm, inverse_hbm, band_hbm,
     snr_hbm, residual_hbm,
     synthesis, lags, forward, series, inverse, band,
-    gathered, own, theirs, spectra, full, turned, snr_out, residual_out,
-    in_sems, out_sems, gather_send, gather_recv, swap_send, swap_recv,
+    gathered, own, theirs, spectra, weights, full, turned, snr_out, residual_out,
+    in_sems, out_sems, line_send, line_recv, relay_send, relay_recv, swap_send, swap_recv,
 ):
     n = lax.axis_size("tmpl")
     me = lax.axis_index("tmpl")
@@ -62,7 +66,7 @@
     loads = [
         pltpu.make_async_copy(src, dst, in_sems.at[i])
         for i, (src, dst) in enumerate([
-            (lags_hbm, lags),
+            (lags_hbm, lags.at[pl.ds(0, length)]),
             (series_hbm, series),
             (synthesis_hbm.at[0], synthesis),
             (forward_hbm.at[section], forward),
@@ -73,18 +77,25 @@
     for load in loads:
         load.start()
 
+    depth, height, breadth = grid
+    place = (me // (height * breadth), me // breadth % height, me % breadth)
+
+    def toward(axis, step):
+        where = [lax.rem(p + step, size) if i == axis else p for i, (p, size) in enumerate(zip(place, grid))]
+        return {"tmpl": (where[0] * height + where[1]) * breadth + where[2]}
+
     barrier = pltpu.get_barrier_semaphore()
-
-    def greet(step, carry):
-        pl.semaphore_signal(
-            barrier, inc=1, device_id={"tmpl": lax.rem(me + step, n)}, device_id_type=MESH
-        )
-        return carry
-
-    lax.fori_loop(1, n, greet, 0)
+    for axis in range(3):
+        for step in range(1, grid[axis]):
+            pl.semaphore_signal(barrier, inc=1, device_id=toward(axis, step), device_id_type=MESH)
     pl.semaphore_signal(barrier, inc=1, device_id={"sect": 1 - section}, device_id_type=MESH)
-
-    wide = jnp.broadcast_to(strain_ref[...], (TAP_GROUP, strain_ref.shape[1]))
+    lags[pl.ds(length, lags.shape[0] - length)] = jnp.zeros(
+        (lags.shape[0] - length,) + lags.shape[1:], jnp.float32
+    )
+
+    signal = strain_ref[...].astype(jnp.float32)
+    signal = jnp.concatenate([signal, jnp.zeros((1, -signal.shape[1] % LANES), jnp.float32)], axis=1)
+    wide = jnp.broadcast_to(signal, (TAP_GROUP, signal.shape[1]))
     width = wide.shape[1]
     hankel = pltpu.roll(wide, width - (TAP_GROUP - 1), 1, stride=1, stride_axis=0)
     hankel = hankel.astype(jnp.bfloat16)
@@ -95,42 +106,21 @@
     for at in range(0, taps, TAP_GROUP):
         bank = dot(filters_ref[:, at : at + TAP_GROUP], flip).astype(jnp.bfloat16)
         basis = basis + dot(bank, hankel[:, at : at + samples])
-    source = lax.broadcasted_iota(jnp.int32, (samples, samples), 0)
-    target = lax.broadcasted_iota(jnp.int32, (samples, samples), 1)
-    target = jnp.where(section == 0, target >> 1, target)
-    hold = jnp.where(source == target, 1.0, 0.0).astype(jnp.bfloat16)
     mine = gathered.at[pl.ds(pl.multiple_of(me * block, block), block)]
-    mine[...] = dot(basis.astype(jnp.bfloat16), hold).astype(jnp.bfloat16)
-
-    pl.semaphore_wait(barrier, n)
-
-    def push(step):
-        return pltpu.make_async_remote_copy(
-            src_ref=mine,
-            dst_ref=mine,
-            send_sem=gather_send.at[step],
-            recv_sem=gather_recv.at[step],
-            device_id={"tmpl": lax.rem(me + step, n)},
-            device_id_type=MESH,
-        )
-
-    def start_push(step, carry):
-        push(step).start()
-        return carry
-
-    def wait_push(step, carry):
-        push(step).wait()
-        return carry
-
-    lax.fori_loop(1, n, start_push, 0)
-
-    loads[0].wait()
-    loads[1].wait()
+    mine[...] = basis.astype(jnp.bfloat16)
+
+    pl.semaphore_wait(barrier, sum(grid) - 3 + 1)
 
     def analyse(c, carry):
         at = pl.ds(pl.multiple_of(c * half, half), half)
-        real = dot(lags[0, at, :], series[...])
-        imag = dot(lags[1, at, :], series[...])
+        a, b = lags[:, 0, at], lags[:, 1, at]
+        real = dot_rows(a.astype(jnp.bfloat16), series[...])
+        imag = dot_rows(b.astype(jnp.bfloat16), series[...])
+        power = a * a + b * b
+        high = power.astype(jnp.bfloat16)
+        low = (power - high.astype(jnp.float32)).astype(jnp.bfloat16)
+        ones = jnp.ones((lags.shape[0], LANES), jnp.bfloat16)
+        weights[at, :] = dot_rows(high, ones) + dot_rows(low, ones)
         for i in range(tiles):
             cos = slice(i * LANES, (i + 1) * LANES)
             sin = slice((tiles + i) * LANES, (tiles + i + 1) * LANES)
@@ -141,10 +131,104 @@
             spectra[3, i, at, :] = as_ + bc
         return carry
 
-    lax.fori_loop(0, chunks, analyse, 0)
+    def gather(used):
+        whole = pl.ds(0, used)
+        parts = (pl.ds(0, used // 2), pl.ds(used // 2, used // 2))
+
+        def spot(offset, columns):
+            where = [lax.rem(p - o + size, size) for p, o, size in zip(place, offset, grid)]
+            index = (where[0] * height + where[1]) * breadth + where[2]
+            return gathered.at[pl.ds(pl.multiple_of(index * block, block), block), columns]
+
+        def line(step):
+            here = spot((0, 0, 0), whole)
+            return pltpu.make_async_remote_copy(
+                src_ref=here, dst_ref=here, send_sem=line_send.at[step], recv_sem=line_recv.at[step],
+                device_id=toward(0, step), device_id_type=MESH,
+            )
+
+        def relay(part, offset, axis, step):
+            here = spot(offset, parts[part])
+            there = tuple(step if i == axis else o for i, o in enumerate(offset))
+            slot = (part,) + there
+            return pltpu.make_async_remote_copy(
+                src_ref=here, dst_ref=here, send_sem=relay_send.at[slot], recv_sem=relay_recv.at[slot],
+                device_id=toward(axis, step), device_id_type=MESH,
+            )
+
+        def arrive_line(step):
+            here = spot((step, 0, 0), whole)
+            pltpu.make_async_remote_copy(
+                src_ref=here, dst_ref=here, send_sem=line_send.at[step], recv_sem=line_recv.at[step],
+                device_id=toward(0, step), device_id_type=MESH,
+            ).wait_recv()
+
+        def arrive(part, offset):
+            here = spot(offset, parts[part])
+            slot = (part,) + offset
+            pltpu.make_async_remote_copy(
+                src_ref=here, dst_ref=here, send_sem=relay_send.at[slot], recv_sem=relay_recv.at[slot],
+                device_id=toward(0, 1), device_id_type=MESH,
+            ).wait_recv()
+
+        sent = []
+
+        def send(copy):
+            copy.start()
+            sent.append(copy)
+
+        def spread(dz):
+            for part in range(2):
+                for axis in ((1, 2) if part == 0 else (2, 1)):
+                    for step in range(1, grid[axis]):
+                        send(relay(part, (dz, 0, 0), axis, step))
+
+        for step in range(1, depth):
+            send(line(step))
+        spread(0)
+        loads[0].wait()
+        loads[1].wait()
+        lax.fori_loop(0, chunks // 2, analyse, 0)
+        for dz in range(1, depth):
+            arrive_line(dz)
+            spread(dz)
+        lax.fori_loop(chunks // 2, chunks * 3 // 4, analyse, 0)
+        for dz in range(depth):
+            for step in range(1, height):
+                arrive(0, (dz, step, 0))
+                for last in range(1, breadth):
+                    send(relay(0, (dz, step, 0), 2, last))
+            for step in range(1, breadth):
+                arrive(1, (dz, 0, step))
+                for last in range(1, height):
+                    send(relay(1, (dz, 0, step), 1, last))
+        lax.fori_loop(chunks * 3 // 4, chunks, analyse, 0)
+        for dz in range(depth):
+            for dy in range(height):
+                for dx in range(1, breadth):
+                    arrive(0, (dz, dy, dx))
+            for dx in range(breadth):
+                for dy in range(1, height):
+                    arrive(1, (dz, dy, dx))
+        for copy in sent:
+            copy.wait_send()
+
+    @pl.when(section == 0)
+    def _():
+        gather(samples // 2)
+        source = lax.broadcasted_iota(jnp.int32, (samples // 2, samples), 0)
+        target = lax.broadcasted_iota(jnp.int32, (samples // 2, samples), 1)
+        hold = jnp.where(source == target // 2, 1.0, 0.0).astype(jnp.bfloat16)
+        for at in range(0, gathered.shape[0], 256):
+            some = slice(at, at + 256)
+            gathered[some, :] = dot(gathered[some, : samples // 2], hold).astype(jnp.bfloat16)
+
+    @pl.when(section != 0)
+    def _():
+        gather(samples)
+
     for load in loads[2:]:
         load.wait()
-    lax.fori_loop(1, n, wait_push, 0)
 
     def swap(c):
         at = pl.ds(pl.multiple_of(c * CHUNK, CHUNK), CHUNK)
@@ -216,7 +300,7 @@
             low.append((power - top.astype(jnp.float32)).astype(jnp.bfloat16))
         energy = dot(jnp.concatenate(high, axis=1), band[...])
         energy = energy + dot(jnp.concatenate(low, axis=1), band[...])
-        weight = weight_ref[to, :]
+        weight = weights[to, :]
         for i in range(share // LANES):
             columns = slice(i * LANES, (i + 1) * LANES)
             tile = section * (share // LANES) + i
@@ -239,7 +323,18 @@
     lax.fori_loop(0, chunks, finish, 0)
 
 
-def local(strain, filters, synthesis, correlation):
+def grid_of(mesh):
+    tmpl = mesh.axis_names.index("tmpl")
+    line = np.moveaxis(mesh.devices, tmpl, 0).reshape(mesh.shape["tmpl"], -1)[:, 0]
+    spots = np.array([device.coords for device in line])[:, ::-1]
+    spots = spots - spots.min(axis=0)
+    grid = tuple(int(size) for size in spots.max(axis=0) + 1)
+    if np.array_equal(spots @ [grid[1] * grid[2], grid[2], 1], np.arange(len(line))):
+        return grid
+    return (len(line), 1, 1)
+
+
+def local(grid, strain, filters, synthesis, correlation):
     sections = lax.axis_size("sect")
     n = lax.axis_size("tmpl")
     block, taps = filters.shape[1:]
@@ -251,22 +346,19 @@
     depth, spectrum = series.shape
     tiles = spectrum // (2 * LANES)
     chunks = rows // CHUNK
-    signal = jnp.pad(strain, ((0, 0), (0, -strain.shape[1] % LANES))).astype(jnp.float32)
-    lags = jnp.pad(correlation, ((0, 0), (0, 0), (0, depth - length))).transpose(1, 0, 2)
-    weight = jnp.sum(correlation * correlation, axis=(1, 2))[:, None]
     vmem = pl.BlockSpec(memory_space=pltpu.VMEM)
     hbm = pl.BlockSpec(memory_space=pl.ANY)
     return pl.pallas_call(
-        functools.partial(kernel, length),
+        functools.partial(kernel, length, grid),
         out_shape=(
             jax.ShapeDtypeStruct((rows, share), jnp.bfloat16),
             jax.ShapeDtypeStruct((groups, share), jnp.float32),
         ),
-        in_specs=[vmem, vmem, hbm, hbm, vmem, hbm, hbm, hbm, hbm],
+        in_specs=[vmem, vmem, hbm, hbm, hbm, hbm, hbm, hbm],
         out_specs=(hbm, hbm),
         scratch_shapes=[
             pltpu.VMEM((rows, n * block), jnp.bfloat16),
-            pltpu.VMEM((2, groups, depth), jnp.bfloat16),
+            pltpu.VMEM((depth, 2, groups), jnp.float32),
             pltpu.VMEM(forward.shape[1:], jnp.bfloat16),
             pltpu.VMEM(series.shape, jnp.bfloat16),
             pltpu.VMEM(inverse.shape[1:], jnp.bfloat16),
@@ -275,22 +367,25 @@
             pltpu.VMEM((rows, samples), jnp.bfloat16),
             pltpu.VMEM((rows, samples), jnp.bfloat16),
             pltpu.VMEM((4, tiles, groups, LANES), jnp.float32),
+            pltpu.VMEM((groups, LANES), jnp.float32),
             pltpu.VMEM((samples // LANES, rows, LANES), jnp.float32),
             pltpu.VMEM((2 * tiles, CHUNK, LANES), jnp.float32),
             pltpu.VMEM((rows, share), jnp.bfloat16),
             pltpu.VMEM((groups, share), jnp.float32),
             pltpu.SemaphoreType.DMA((6,)),
             pltpu.SemaphoreType.DMA((2, chunks)),
-            pltpu.SemaphoreType.DMA((n,)),
-            pltpu.SemaphoreType.DMA((n,)),
+            pltpu.SemaphoreType.DMA((grid[0],)),
+            pltpu.SemaphoreType.DMA((grid[0],)),
+            pltpu.SemaphoreType.DMA((2,) + grid),
+            pltpu.SemaphoreType.DMA((2,) + grid),
             pltpu.SemaphoreType.DMA((chunks,)),
             pltpu.SemaphoreType.DMA((chunks,)),
         ],
         compiler_params=pltpu.CompilerParams(
-            collective_id=0, has_side_effects=True, vmem_limit_bytes=56 * 2**20
+            collective_id=0, has_side_effects=True, vmem_limit_bytes=36 * 2**20
         ),
     )(
-        signal, filters[0], synthesis, lags.astype(jnp.bfloat16), weight,
+        strain, filters[0], synthesis, correlation.transpose(2, 1, 0),
         forward, series, inverse, band,
     )
 
@@ -303,7 +398,7 @@
         P("tmpl", None, None),
     )
     return jax.shard_map(
-        local,
+        functools.partial(local, grid_of(mesh)),
         mesh=mesh,
         in_specs=placed,
         out_specs=(P("tmpl", "sect"), P("tmpl", "sect")),

time: 55.5 us -> 48 us (0.86)
  the two profiles are of different devices: /device:TPU:15 before, /device:TPU:0 now
where the time goes in v2:
time: 48 us; the launch traced here: 47.6 us
  Pallas kernels  34.7 us (72%)
  local copies, waits for them, and re-layouts  12.2 us (25%)
  between operations  0.65 us (1%)
    pallas_call x1, Pallas kernels, local(): pl.pallas_call(functools.partial(kernel, length, grid), out_shape=(jax.Sh...  34.7 us
    unnamed x18, local copies, waits for them, and re-layouts  12.2 us

profile of v2, /device:TPU:0, one launch (start us, length us, event | category | flops | bytes accessed | tf_op | source)
XLA Modules:
  0.0 47.6 jit_solution(167844332848232651)
XLA Ops:
  0.6 0.0 copy-start
  0.6 2.2 %copy-done = bf16[1,2048,1024]{2,1,0:T(8,128)(2,1)S(1)} copy-done((bf16[1,2048,1024]{2,1,0:T(8,128)(2,1)S(1)}, bf16[1,2048,1024]{2,1,0:T(8,128)(2,1)}, u32[]{:S(2)}) %copy-start) | copy-done | bytes 4194328
  2.8 0.0 copy-start.1
  2.8 1.8 %copy-done.1 = f32[1024,2,351]{0,1,2:T(2,128)S(1)} copy-done((f32[1024,2,351]{0,1,2:T(2,128)S(1)}, f32[1024,2,351]{0,1,2:T(2,128)}, u32[]{:S(2)}) %copy-start.1) | copy-done | bytes 2875416
  4.6 0.0 copy-start.2
  4.6 1.4 %copy-done.2 = bf16[2,512,768]{2,1,0:T(8,128)(2,1)S(1)} copy-done((bf16[2,512,768]{2,1,0:T(8,128)(2,1)S(1)}, bf16[2,512,768]{2,1,0:T(8,128)(2,1)}, u32[]{:S(2)}) %copy-start.2) | copy-done | bytes 1572888
  6.0 0.0 copy-start.3
  6.0 1.1 %copy-done.3 = bf16[2,768,256]{2,1,0:T(8,128)(2,1)S(1)} copy-done((bf16[2,768,256]{2,1,0:T(8,128)(2,1)S(1)}, bf16[2,768,256]{2,1,0:T(8,128)(2,1)}, u32[]{:S(2)}) %copy-start.3) | copy-done | bytes 786456
  7.2 0.0 copy-start.4
  7.2 1.1 %copy-done.4 = bf16[384,768]{1,0:T(8,128)(2,1)S(1)} copy-done((bf16[384,768]{1,0:T(8,128)(2,1)S(1)}, bf16[384,768]{1,0:T(8,128)(2,1)}, u32[]{:S(2)}) %copy-start.4) | copy-done | bytes 589848
  8.2 0.0 copy-start.5
  8.2 1.0 %copy-done.5 = bf16[2,512,256]{2,1,0:T(8,128)(2,1)S(1)} copy-done((bf16[2,512,256]{2,1,0:T(8,128)(2,1)S(1)}, bf16[2,512,256]{2,1,0:T(8,128)(2,1)}, u32[]{:S(2)}) %copy-start.5) | copy-done | bytes 524312
  9.3 0.0 copy-start.6
  9.3 0.9 %copy-done.6 = bf16[1,64,1024]{2,1,0:T(8,128)(2,1)S(1)} copy-done((bf16[1,64,1024]{2,1,0:T(8,128)(2,1)S(1)}, bf16[1,64,1024]{2,1,0:T(8,128)(2,1)}, u32[]{:S(2)}) %copy-start.6) | copy-done | bytes 131096
  10.2 0.0 copy-start.7
  10.2 0.7 %copy-done.7 = bf16[1,1535]{1,0:T(2,128)(2,1)S(1)} copy-done((bf16[1,1535]{1,0:T(2,128)(2,1)S(1)}, bf16[1,1535]{1,0:T(2,128)(2,1)}, u32[]{:S(2)}) %copy-start.7) | copy-done | bytes 3094
  10.9 34.7 %shard_map.95 = (bf16[2048,256]{1,0:T(8,128)(2,1)S(1)}, f32[1024,256]{1,0:T(8,128)S(1)}) custom-call(bf16[1,1535]{1,0:T(2,128)(2,1)S(1)} %copy-done.7, bf16[64,1024]{1,0:T(8,128)(2,1)S(1)} %bitcast.3, bf16[1,2048,1024]{2,1,0:T(8,128)(2,1)S(1)} %copy-done, f32[351,2,1024]{2,1,0:T(2,128)S(1)} %bitcast.2, bf16[2,512,768]{2,1,0:T(8,128)(2,1)S(1)} %copy-done.2, ...), custom_call_target="tpu_custom_call" | custom-call | tf_op jit(solution)/shard_map/pallas_call | solution.py:351
  45.6 1.0 %copy.12 = bf16[2048,256]{1,0:T(8,128)(2,1)} copy(bf16[2048,256]{1,0:T(8,128)(2,1)S(1)} %get-tuple-element.4) | data formatting | bytes 2097152
  46.6 1.0 %copy.13 = f32[1024,256]{1,0:T(8,128)} copy(f32[1024,256]{1,0:T(8,128)S(1)} %get-tuple-element.5) | data formatting | bytes 2097152
Async XLA Ops:
  0.6 2.2 %copy-start = (bf16[1,2048,1024]{2,1,0:T(8,128)(2,1)S(1)}, bf16[1,2048,1024]{2,1,0:T(8,128)(2,1)}, u32[]{:S(2)}) copy-start(bf16[1,2048,1024]{2,1,0:T(8,128)(2,1)} %synthesis_hbm.1) | copy-start | bytes 12582916
  2.8 1.8 %copy-start.1 = (f32[1024,2,351]{0,1,2:T(2,128)S(1)}, f32[1024,2,351]{0,1,2:T(2,128)}, u32[]{:S(2)}) copy-start(f32[1024,2,351]{0,1,2:T(2,128)} %param.11) | copy-start | bytes 8626180
  4.6 1.4 %copy-start.2 = (bf16[2,512,768]{2,1,0:T(8,128)(2,1)S(1)}, bf16[2,512,768]{2,1,0:T(8,128)(2,1)}, u32[]{:S(2)}) copy-start(bf16[2,512,768]{2,1,0:T(8,128)(2,1)} %constant.8.clone.forward_hbm) | copy-start | bytes 4718596
  6.0 1.1 %copy-start.3 = (bf16[2,768,256]{2,1,0:T(8,128)(2,1)S(1)}, bf16[2,768,256]{2,1,0:T(8,128)(2,1)}, u32[]{:S(2)}) copy-start(bf16[2,768,256]{2,1,0:T(8,128)(2,1)} %constant.10.clone.inverse_hbm) | copy-start | bytes 2359300
  7.2 1.1 %copy-start.4 = (bf16[384,768]{1,0:T(8,128)(2,1)S(1)}, bf16[384,768]{1,0:T(8,128)(2,1)}, u32[]{:S(2)}) copy-start(bf16[384,768]{1,0:T(8,128)(2,1)} %constant.9.clone.series_hbm) | copy-start | bytes 1769476
  8.2 1.0 %copy-start.5 = (bf16[2,512,256]{2,1,0:T(8,128)(2,1)S(1)}, bf16[2,512,256]{2,1,0:T(8,128)(2,1)}, u32[]{:S(2)}) copy-start(bf16[2,512,256]{2,1,0:T(8,128)(2,1)} %constant.11.clone.band_hbm) | copy-start | bytes 1572868
  9.3 0.9 %copy-start.6 = (bf16[1,64,1024]{2,1,0:T(8,128)(2,1)S(1)}, bf16[1,64,1024]{2,1,0:T(8,128)(2,1)}, u32[]{:S(2)}) copy-start(bf16[1,64,1024]{2,1,0:T(8,128)(2,1)} %param.9) | copy-start | bytes 393220
  10.2 0.7 %copy-start.7 = (bf16[1,1535]{1,0:T(2,128)(2,1)S(1)}, bf16[1,1535]{1,0:T(2,128)(2,1)}, u32[]{:S(2)}) copy-start(bf16[1,1535]{1,0:T(2,128)(2,1)} %strain_ref.1) | copy-start | bytes 9214

commit v3 on v2

--- a/solution.py
+++ b/solution.py
@@ -45,11 +45,11 @@
 
 def kernel(
     length, grid,
-    strain_ref, filters_ref, synthesis_hbm, lags_hbm,
+    strain_hbm, filters_hbm, synthesis_hbm, lags_hbm,
     forward_hbm, series_hbm, inverse_hbm, band_hbm,
     snr_hbm, residual_hbm,
-    synthesis, lags, forward, series, inverse, band,
-    gathered, own, theirs, spectra, weights, full, turned, snr_out, residual_out,
+    strain_ref, filters_ref, synthesis, lags, forward, series, inverse, band,
+    gathered, own, theirs, spectra, weights, kept, full, snr_out, residual_out,
     in_sems, out_sems, line_send, line_recv, relay_send, relay_recv, swap_send, swap_recv,
 ):
     n = lax.axis_size("tmpl")
@@ -66,6 +66,8 @@
     loads = [
         pltpu.make_async_copy(src, dst, in_sems.at[i])
         for i, (src, dst) in enumerate([
+            (strain_hbm, strain_ref),
+            (filters_hbm, filters_ref),
             (lags_hbm, lags.at[pl.ds(0, length)]),
             (series_hbm, series),
             (synthesis_hbm.at[0], synthesis),
@@ -93,6 +95,8 @@
         (lags.shape[0] - length,) + lags.shape[1:], jnp.float32
     )
 
+    loads[0].wait()
+    loads[1].wait()
     signal = strain_ref[...].astype(jnp.float32)
     signal = jnp.concatenate([signal, jnp.zeros((1, -signal.shape[1] % LANES), jnp.float32)], axis=1)
     wide = jnp.broadcast_to(signal, (TAP_GROUP, signal.shape[1]))
@@ -186,8 +190,8 @@
         for step in range(1, depth):
             send(line(step))
         spread(0)
-        loads[0].wait()
-        loads[1].wait()
+        loads[2].wait()
+        loads[3].wait()
         lax.fori_loop(0, chunks // 2, analyse, 0)
         for dz in range(1, depth):
             arrive_line(dz)
@@ -227,7 +231,7 @@
     def _():
         gather(samples)
 
-    for load in loads[2:]:
+    for load in loads[4:]:
         load.wait()
 
     def swap(c):
@@ -241,16 +245,12 @@
             device_id_type=MESH,
         )
 
-    def reconstruct(c, carry):
+    def multiply(c):
         at = pl.ds(pl.multiple_of(c * CHUNK, CHUNK), CHUNK)
         value = dot(synthesis[at, :], gathered[...])
         own[at, :] = value.astype(jnp.bfloat16)
-        swap(c).start()
         for i in range(samples // LANES):
-            full[i, at, :] = value[:, i * LANES : (i + 1) * LANES]
-        return carry
-
-    lax.fori_loop(0, chunks, reconstruct, 0)
+            kept[i, at, :] = value[:, i * LANES : (i + 1) * LANES]
 
     def emit(c):
         at = pl.ds(pl.multiple_of(c * CHUNK, CHUNK), CHUNK)
@@ -260,26 +260,31 @@
             pltpu.make_async_copy(residual_out.at[to], residual_hbm.at[to], out_sems.at[1, c]),
         )
 
-    def resolve(c, carry):
-        start = pl.multiple_of(c * CHUNK, CHUNK)
-        at = pl.ds(start, CHUNK)
+    def resolve(c):
+        at = pl.ds(pl.multiple_of(c * CHUNK, CHUNK), CHUNK)
         to = pl.ds(pl.multiple_of(c * half, half), half)
-        even = pl.ds(start, half, stride=2)
-        odd = pl.ds(start + 1, half, stride=2)
-        swap(c).wait()
-        parts = []
+        even, odd = pl.ds(0, half, stride=2), pl.ds(1, half, stride=2)
         for i in range(samples // LANES):
-            part = full[i, at, :] + theirs[at, i * LANES : (i + 1) * LANES].astype(jnp.float32)
-            full[i, at, :] = part
-            parts.append(part.astype(jnp.bfloat16))
-        spectrum = dot(jnp.concatenate(parts, axis=1), forward[...])
-        for i in range(2 * tiles):
-            turned[i] = spectrum[:, i * LANES : (i + 1) * LANES]
-        evens, odds = pl.ds(0, half, stride=2), pl.ds(1, half, stride=2)
+            full[i] = kept[i, at, :] + theirs[at, i * LANES : (i + 1) * LANES].astype(jnp.float32)
+        xs_in, ys_in, high, low = [], [], [], []
+        for i in range(samples // LANES):
+            x, y = full[i, even, :], full[i, odd, :]
+            xs_in.append(x.astype(jnp.bfloat16))
+            ys_in.append(y.astype(jnp.bfloat16))
+            power = x * x + y * y
+            top = power.astype(jnp.bfloat16)
+            high.append(top)
+            low.append((power - top.astype(jnp.float32)).astype(jnp.bfloat16))
+        xs_in, ys_in = jnp.concatenate(xs_in, axis=1), jnp.concatenate(ys_in, axis=1)
+        spectrum = dot(jnp.concatenate([xs_in, ys_in], axis=0), forward[...])
+        energy = dot(jnp.concatenate(high, axis=1), band[...])
+        energy = energy + dot(jnp.concatenate(low, axis=1), band[...])
         ur, ui, vr, vi = [], [], [], []
         for i in range(tiles):
-            xc, yc = turned[i, evens, :], turned[i, odds, :]
-            xs, ys = turned[tiles + i, evens, :], turned[tiles + i, odds, :]
+            cos = slice(i * LANES, (i + 1) * LANES)
+            sin = slice((tiles + i) * LANES, (tiles + i + 1) * LANES)
+            xc, yc = spectrum[:half, cos], spectrum[half:, cos]
+            xs, ys = spectrum[:half, sin], spectrum[half:, sin]
             pr, pi = spectra[0, i, to, :], spectra[1, i, to, :]
             mr, mi = spectra[2, i, to, :], spectra[3, i, to, :]
             zpr, zpi, zmr, zmi = xc + ys, yc - xs, xc - ys, -xs - yc
@@ -291,29 +296,41 @@
             vi.append((wmr - wpr).astype(jnp.bfloat16))
         u = dot(jnp.concatenate(ur + ui, axis=1), inverse[...])
         v = dot(jnp.concatenate(vr + vi, axis=1), inverse[...])
-        high, low = [], []
-        for i in range(samples // LANES):
-            x, y = full[i, even, :], full[i, odd, :]
-            power = x * x + y * y
-            top = power.astype(jnp.bfloat16)
-            high.append(top)
-            low.append((power - top.astype(jnp.float32)).astype(jnp.bfloat16))
-        energy = dot(jnp.concatenate(high, axis=1), band[...])
-        energy = energy + dot(jnp.concatenate(low, axis=1), band[...])
         weight = weights[to, :]
         for i in range(share // LANES):
             columns = slice(i * LANES, (i + 1) * LANES)
             tile = section * (share // LANES) + i
-            snr_out[at, columns] = full[tile, at, :].astype(jnp.bfloat16)
+            snr_out[at, columns] = full[tile].astype(jnp.bfloat16)
             x, y = full[tile, even, :], full[tile, odd, :]
             cross = x * u[:, columns] + y * v[:, columns]
             value = energy[:, columns] - 2.0 * cross + (x * x + y * y) * weight
             residual_out[to, columns] = value / (2.0 * length)
+    ahead = min(2, chunks)
+
+    def lead(c, carry):
+        multiply(c)
+        swap(c).start()
+        return carry
+
+    def both(c, carry):
+        swap(c).wait()
+        multiply(c + ahead)
+        resolve(c)
+        swap(c + ahead).start()
         for copy in emit(c):
             copy.start()
         return carry
 
-    lax.fori_loop(0, chunks, resolve, 0)
+    def trail(c, carry):
+        swap(c).wait()
+        resolve(c)
+        for copy in emit(c):
+            copy.start()
+        return carry
+
+    lax.fori_loop(0, ahead, lead, 0)
+    lax.fori_loop(0, chunks - ahead, both, 0)
+    lax.fori_loop(chunks - ahead, chunks, trail, 0)
 
     def finish(c, carry):
         for copy in emit(c):
@@ -346,7 +363,6 @@
     depth, spectrum = series.shape
     tiles = spectrum // (2 * LANES)
     chunks = rows // CHUNK
-    vmem = pl.BlockSpec(memory_space=pltpu.VMEM)
     hbm = pl.BlockSpec(memory_space=pl.ANY)
     return pl.pallas_call(
         functools.partial(kernel, length, grid),
@@ -354,9 +370,11 @@
             jax.ShapeDtypeStruct((rows, share), jnp.bfloat16),
             jax.ShapeDtypeStruct((groups, share), jnp.float32),
         ),
-        in_specs=[vmem, vmem, hbm, hbm, hbm, hbm, hbm, hbm],
+        in_specs=[pl.BlockSpec(memory_space=pltpu.HBM)] * 8,
         out_specs=(hbm, hbm),
         scratch_shapes=[
+            pltpu.VMEM(strain.shape, jnp.bfloat16),
+            pltpu.VMEM((block, taps), jnp.bfloat16),
             pltpu.VMEM((rows, n * block), jnp.bfloat16),
             pltpu.VMEM((depth, 2, groups), jnp.float32),
             pltpu.VMEM(forward.shape[1:], jnp.bfloat16),
@@ -369,10 +387,10 @@
             pltpu.VMEM((4, tiles, groups, LANES), jnp.float32),
             pltpu.VMEM((groups, LANES), jnp.float32),
             pltpu.VMEM((samples // LANES, rows, LANES), jnp.float32),
-            pltpu.VMEM((2 * tiles, CHUNK, LANES), jnp.float32),
+            pltpu.VMEM((samples // LANES, CHUNK, LANES), jnp.float32),
             pltpu.VMEM((rows, share), jnp.bfloat16),
             pltpu.VMEM((groups, share), jnp.float32),
-            pltpu.SemaphoreType.DMA((6,)),
+            pltpu.SemaphoreType.DMA((8,)),
             pltpu.SemaphoreType.DMA((2, chunks)),
             pltpu.SemaphoreType.DMA((grid[0],)),
             pltpu.SemaphoreType.DMA((grid[0],)),

time: 48 us -> 47.4 us (0.987)
  Pallas kernels: 34.7 us -> 34.1 us
    pallas_call x1, Pallas kernels: 34.7 us -> 34.1 us  [local(): pl.pallas_call(functools.partial(kernel, length, grid), out_shape=(jax.Sh...]
where the time goes in v3:
time: 47.4 us; the launch traced here: 46.9 us
  Pallas kernels  34.1 us (72%)
  local copies, waits for them, and re-layouts  12.2 us (26%)
  between operations  0.65 us (1%)
    pallas_call x1, Pallas kernels, local(): pl.pallas_call(functools.partial(kernel, length, grid), out_shape=(jax.Sh...  34.1 us
    unnamed x18, local copies, waits for them, and re-layouts  12.2 us

profile of v3, /device:TPU:0, one launch (start us, length us, event | category | flops | bytes accessed | tf_op | source)
XLA Modules:
  0.0 46.9 jit_solution(4604335812377655656)
XLA Ops:
  0.6 0.0 copy-start
  0.6 2.2 %copy-done = bf16[1,2048,1024]{2,1,0:T(8,128)(2,1)S(1)} copy-done((bf16[1,2048,1024]{2,1,0:T(8,128)(2,1)S(1)}, bf16[1,2048,1024]{2,1,0:T(8,128)(2,1)}, u32[]{:S(2)}) %copy-start) | copy-done | bytes 4194328
  2.8 0.0 copy-start.1
  2.8 1.8 %copy-done.1 = f32[1024,2,351]{0,1,2:T(2,128)S(1)} copy-done((f32[1024,2,351]{0,1,2:T(2,128)S(1)}, f32[1024,2,351]{0,1,2:T(2,128)}, u32[]{:S(2)}) %copy-start.1) | copy-done | bytes 2875416
  4.6 0.0 copy-start.2
  4.6 1.4 %copy-done.2 = bf16[2,512,768]{2,1,0:T(8,128)(2,1)S(1)} copy-done((bf16[2,512,768]{2,1,0:T(8,128)(2,1)S(1)}, bf16[2,512,768]{2,1,0:T(8,128)(2,1)}, u32[]{:S(2)}) %copy-start.2) | copy-done | bytes 1572888
  6.0 0.0 copy-start.3
  6.0 1.1 %copy-done.3 = bf16[2,768,256]{2,1,0:T(8,128)(2,1)S(1)} copy-done((bf16[2,768,256]{2,1,0:T(8,128)(2,1)S(1)}, bf16[2,768,256]{2,1,0:T(8,128)(2,1)}, u32[]{:S(2)}) %copy-start.3) | copy-done | bytes 786456
  7.2 0.0 copy-start.4
  7.2 1.1 %copy-done.4 = bf16[384,768]{1,0:T(8,128)(2,1)S(1)} copy-done((bf16[384,768]{1,0:T(8,128)(2,1)S(1)}, bf16[384,768]{1,0:T(8,128)(2,1)}, u32[]{:S(2)}) %copy-start.4) | copy-done | bytes 589848
  8.2 0.0 copy-start.5
  8.2 1.0 %copy-done.5 = bf16[2,512,256]{2,1,0:T(8,128)(2,1)S(1)} copy-done((bf16[2,512,256]{2,1,0:T(8,128)(2,1)S(1)}, bf16[2,512,256]{2,1,0:T(8,128)(2,1)}, u32[]{:S(2)}) %copy-start.5) | copy-done | bytes 524312
  9.3 0.0 copy-start.6
  9.3 0.9 %copy-done.6 = bf16[1,64,1024]{2,1,0:T(8,128)(2,1)S(1)} copy-done((bf16[1,64,1024]{2,1,0:T(8,128)(2,1)S(1)}, bf16[1,64,1024]{2,1,0:T(8,128)(2,1)}, u32[]{:S(2)}) %copy-start.6) | copy-done | bytes 131096
  10.2 0.0 copy-start.7
  10.2 0.7 %copy-done.7 = bf16[1,1535]{1,0:T(2,128)(2,1)S(1)} copy-done((bf16[1,1535]{1,0:T(2,128)(2,1)S(1)}, bf16[1,1535]{1,0:T(2,128)(2,1)}, u32[]{:S(2)}) %copy-start.7) | copy-done | bytes 3094
  10.9 34.1 %shard_map.95 = (bf16[2048,256]{1,0:T(8,128)(2,1)S(1)}, f32[1024,256]{1,0:T(8,128)S(1)}) custom-call(bf16[1,1535]{1,0:T(2,128)(2,1)S(1)} %copy-done.7, bf16[64,1024]{1,0:T(8,128)(2,1)S(1)} %bitcast.3, bf16[1,2048,1024]{2,1,0:T(8,128)(2,1)S(1)} %copy-done, f32[351,2,1024]{2,1,0:T(2,128)S(1)} %bitcast.2, bf16[2,512,768]{2,1,0:T(8,128)(2,1)S(1)} %copy-done.2, ...), custom_call_target="tpu_custom_call" | custom-call | tf_op jit(solution)/shard_map/pallas_call | solution.py:367
  45.0 1.0 %copy.12 = bf16[2048,256]{1,0:T(8,128)(2,1)} copy(bf16[2048,256]{1,0:T(8,128)(2,1)S(1)} %get-tuple-element.4) | data formatting | bytes 2097152
  46.0 1.0 %copy.13 = f32[1024,256]{1,0:T(8,128)} copy(f32[1024,256]{1,0:T(8,128)S(1)} %get-tuple-element.5) | data formatting | bytes 2097152
Async XLA Ops:
  0.6 2.2 %copy-start = (bf16[1,2048,1024]{2,1,0:T(8,128)(2,1)S(1)}, bf16[1,2048,1024]{2,1,0:T(8,128)(2,1)}, u32[]{:S(2)}) copy-start(bf16[1,2048,1024]{2,1,0:T(8,128)(2,1)} %synthesis_hbm.1) | copy-start | bytes 12582916
  2.8 1.8 %copy-start.1 = (f32[1024,2,351]{0,1,2:T(2,128)S(1)}, f32[1024,2,351]{0,1,2:T(2,128)}, u32[]{:S(2)}) copy-start(f32[1024,2,351]{0,1,2:T(2,128)} %param.11) | copy-start | bytes 8626180
  4.6 1.4 %copy-start.2 = (bf16[2,512,768]{2,1,0:T(8,128)(2,1)S(1)}, bf16[2,512,768]{2,1,0:T(8,128)(2,1)}, u32[]{:S(2)}) copy-start(bf16[2,512,768]{2,1,0:T(8,128)(2,1)} %constant.8.clone.forward_hbm) | copy-start | bytes 4718596
  6.0 1.1 %copy-start.3 = (bf16[2,768,256]{2,1,0:T(8,128)(2,1)S(1)}, bf16[2,768,256]{2,1,0:T(8,128)(2,1)}, u32[]{:S(2)}) copy-start(bf16[2,768,256]{2,1,0:T(8,128)(2,1)} %constant.10.clone.inverse_hbm) | copy-start | bytes 2359300
  7.2 1.1 %copy-start.4 = (bf16[384,768]{1,0:T(8,128)(2,1)S(1)}, bf16[384,768]{1,0:T(8,128)(2,1)}, u32[]{:S(2)}) copy-start(bf16[384,768]{1,0:T(8,128)(2,1)} %constant.9.clone.series_hbm) | copy-start | bytes 1769476
  8.2 1.0 %copy-start.5 = (bf16[2,512,256]{2,1,0:T(8,128)(2,1)S(1)}, bf16[2,512,256]{2,1,0:T(8,128)(2,1)}, u32[]{:S(2)}) copy-start(bf16[2,512,256]{2,1,0:T(8,128)(2,1)} %constant.11.clone.band_hbm) | copy-start | bytes 1572868
  9.3 0.9 %copy-start.6 = (bf16[1,64,1024]{2,1,0:T(8,128)(2,1)S(1)}, bf16[1,64,1024]{2,1,0:T(8,128)(2,1)}, u32[]{:S(2)}) copy-start(bf16[1,64,1024]{2,1,0:T(8,128)(2,1)} %param.9) | copy-start | bytes 393220
  10.2 0.7 %copy-start.7 = (bf16[1,1535]{1,0:T(2,128)(2,1)S(1)}, bf16[1,1535]{1,0:T(2,128)(2,1)}, u32[]{:S(2)}) copy-start(bf16[1,1535]{1,0:T(2,128)(2,1)} %strain_hbm.1) | copy-start | bytes 9214

commit v4 on v3

--- a/solution.py
+++ b/solution.py
@@ -9,7 +9,8 @@
 from jax.sharding import PartitionSpec as P
 
 LANES = 128
-TAP_GROUP = 256
+TAP_GROUP = 128
+SUBLANES = 8
 CHUNK = 256
 MESH = pl.DeviceIdType.MESH
 
@@ -68,7 +69,8 @@
         for i, (src, dst) in enumerate([
             (strain_hbm, strain_ref),
             (filters_hbm, filters_ref),
-            (lags_hbm, lags.at[pl.ds(0, length)]),
+            (lags_hbm.at[:, 0], lags.at[0]),
+            (lags_hbm.at[:, 1], lags.at[1]),
             (series_hbm, series),
             (synthesis_hbm.at[0], synthesis),
             (forward_hbm.at[section], forward),
@@ -91,25 +93,20 @@
         for step in range(1, grid[axis]):
             pl.semaphore_signal(barrier, inc=1, device_id=toward(axis, step), device_id_type=MESH)
     pl.semaphore_signal(barrier, inc=1, device_id={"sect": 1 - section}, device_id_type=MESH)
-    lags[pl.ds(length, lags.shape[0] - length)] = jnp.zeros(
-        (lags.shape[0] - length,) + lags.shape[1:], jnp.float32
-    )
-
     loads[0].wait()
     loads[1].wait()
     signal = strain_ref[...].astype(jnp.float32)
     signal = jnp.concatenate([signal, jnp.zeros((1, -signal.shape[1] % LANES), jnp.float32)], axis=1)
-    wide = jnp.broadcast_to(signal, (TAP_GROUP, signal.shape[1]))
-    width = wide.shape[1]
-    hankel = pltpu.roll(wide, width - (TAP_GROUP - 1), 1, stride=1, stride_axis=0)
-    hankel = hankel.astype(jnp.bfloat16)
-    down = lax.broadcasted_iota(jnp.int32, (TAP_GROUP, TAP_GROUP), 0)
-    across = lax.broadcasted_iota(jnp.int32, (TAP_GROUP, TAP_GROUP), 1)
-    flip = jnp.where(down + across == TAP_GROUP - 1, 1.0, 0.0).astype(jnp.bfloat16)
+    width = signal.shape[1]
+    shifted = [signal] + [pltpu.roll(signal, width - i, 1) for i in range(1, SUBLANES)]
+    shifted = jnp.concatenate(shifted, axis=0)
+    hankel = [shifted] + [
+        pltpu.roll(shifted, width - i, 1) for i in range(SUBLANES, TAP_GROUP, SUBLANES)
+    ]
+    hankel = jnp.concatenate(hankel, axis=0).astype(jnp.bfloat16)
     basis = jnp.zeros((block, samples), jnp.float32)
     for at in range(0, taps, TAP_GROUP):
-        bank = dot(filters_ref[:, at : at + TAP_GROUP], flip).astype(jnp.bfloat16)
-        basis = basis + dot(bank, hankel[:, at : at + samples])
+        basis = basis + dot(filters_ref[:, at : at + TAP_GROUP], hankel[:, at : at + samples])
     mine = gathered.at[pl.ds(pl.multiple_of(me * block, block), block)]
     mine[...] = basis.astype(jnp.bfloat16)
 
@@ -117,13 +114,13 @@
 
     def analyse(c, carry):
         at = pl.ds(pl.multiple_of(c * half, half), half)
-        a, b = lags[:, 0, at], lags[:, 1, at]
-        real = dot_rows(a.astype(jnp.bfloat16), series[...])
-        imag = dot_rows(b.astype(jnp.bfloat16), series[...])
+        a, b = lags[0, :, at], lags[1, :, at]
+        real = dot_rows(a.astype(jnp.bfloat16), series[pl.ds(0, length), :])
+        imag = dot_rows(b.astype(jnp.bfloat16), series[pl.ds(0, length), :])
         power = a * a + b * b
         high = power.astype(jnp.bfloat16)
         low = (power - high.astype(jnp.float32)).astype(jnp.bfloat16)
-        ones = jnp.ones((lags.shape[0], LANES), jnp.bfloat16)
+        ones = jnp.ones((length, LANES), jnp.bfloat16)
         weights[at, :] = dot_rows(high, ones) + dot_rows(low, ones)
         for i in range(tiles):
             cos = slice(i * LANES, (i + 1) * LANES)
@@ -192,6 +189,7 @@
         spread(0)
         loads[2].wait()
         loads[3].wait()
+        loads[4].wait()
         lax.fori_loop(0, chunks // 2, analyse, 0)
         for dz in range(1, depth):
             arrive_line(dz)
@@ -231,7 +229,7 @@
     def _():
         gather(samples)
 
-    for load in loads[4:]:
+    for load in loads[5:]:
         load.wait()
 
     def swap(c):
@@ -277,8 +275,9 @@
             low.append((power - top.astype(jnp.float32)).astype(jnp.bfloat16))
         xs_in, ys_in = jnp.concatenate(xs_in, axis=1), jnp.concatenate(ys_in, axis=1)
         spectrum = dot(jnp.concatenate([xs_in, ys_in], axis=0), forward[...])
-        energy = dot(jnp.concatenate(high, axis=1), band[...])
-        energy = energy + dot(jnp.concatenate(low, axis=1), band[...])
+        high, low = jnp.concatenate(high, axis=1), jnp.concatenate(low, axis=1)
+        energy = dot(jnp.concatenate([high, low], axis=0), band[...])
+        energy = energy[:half] + energy[half:]
         ur, ui, vr, vi = [], [], [], []
         for i in range(tiles):
             cos = slice(i * LANES, (i + 1) * LANES)
@@ -294,8 +293,11 @@
             ui.append((wpi + wmi).astype(jnp.bfloat16))
             vr.append((wpi - wmi).astype(jnp.bfloat16))
             vi.append((wmr - wpr).astype(jnp.bfloat16))
-        u = dot(jnp.concatenate(ur + ui, axis=1), inverse[...])
-        v = dot(jnp.concatenate(vr + vi, axis=1), inverse[...])
+        turned = jnp.concatenate(
+            [jnp.concatenate(ur + ui, axis=1), jnp.concatenate(vr + vi, axis=1)], axis=0
+        )
+        turned = dot(turned, inverse[...])
+        u, v = turned[:half], turned[half:]
         weight = weights[to, :]
         for i in range(share // LANES):
             columns = slice(i * LANES, (i + 1) * LANES)
@@ -376,7 +378,7 @@
             pltpu.VMEM(strain.shape, jnp.bfloat16),
             pltpu.VMEM((block, taps), jnp.bfloat16),
             pltpu.VMEM((rows, n * block), jnp.bfloat16),
-            pltpu.VMEM((depth, 2, groups), jnp.float32),
+            pltpu.VMEM((2, length, groups), jnp.float32),
             pltpu.VMEM(forward.shape[1:], jnp.bfloat16),
             pltpu.VMEM(series.shape, jnp.bfloat16),
             pltpu.VMEM(inverse.shape[1:], jnp.bfloat16),
@@ -390,7 +392,7 @@
             pltpu.VMEM((samples // LANES, CHUNK, LANES), jnp.float32),
             pltpu.VMEM((rows, share), jnp.bfloat16),
             pltpu.VMEM((groups, share), jnp.float32),
-            pltpu.SemaphoreType.DMA((8,)),
+            pltpu.SemaphoreType.DMA((9,)),
             pltpu.SemaphoreType.DMA((2, chunks)),
             pltpu.SemaphoreType.DMA((grid[0],)),
             pltpu.SemaphoreType.DMA((grid[0],)),
@@ -400,7 +402,7 @@
             pltpu.SemaphoreType.DMA((chunks,)),
         ],
         compiler_params=pltpu.CompilerParams(
-            collective_id=0, has_side_effects=True, vmem_limit_bytes=36 * 2**20
+            collective_id=0, has_side_effects=True, vmem_limit_bytes=56 * 2**20
         ),
     )(
         strain, filters[0], synthesis, correlation.transpose(2, 1, 0),

time: 47.4 us -> 36.7 us (0.77)
  local copies, waits for them, and re-layouts: 12.2 us -> 4.52 us
  Pallas kernels: 34.1 us -> 31.3 us
    unnamed x18 -> x2, local copies, waits for them, and re-layouts: 12.2 us -> 4.52 us
    pallas_call x1, Pallas kernels: 34.1 us -> 31.3 us  [local(): pl.pallas_call(functools.partial(kernel, length, grid), out_shape=(jax.Sh...]
where the time goes in v4:
time: 36.7 us; the launch traced here: 36.5 us
  Pallas kernels  31.3 us (85%)
  local copies, waits for them, and re-layouts  4.52 us (12%)
  between operations  0.64 us (2%)
    pallas_call x1, Pallas kernels, local(): pl.pallas_call(functools.partial(kernel, length, grid), out_shape=(jax.Sh...  31.3 us
    unnamed x2, local copies, waits for them, and re-layouts  4.52 us

profile of v4, /device:TPU:0, one launch (start us, length us, event | category | flops | bytes accessed | tf_op | source)
XLA Modules:
  0.0 36.5 jit_solution(5602659940857803545)
XLA Ops:
  0.6 31.3 %shard_map.95 = (bf16[2048,256]{1,0:T(8,128)(2,1)}, f32[1024,256]{1,0:T(8,128)}) custom-call(bf16[1,1535]{1,0:T(2,128)(2,1)} %strain_hbm.1, bf16[64,1024]{1,0:T(8,128)(2,1)} %bitcast.3, bf16[1,2048,1024]{2,1,0:T(8,128)(2,1)} %synthesis_hbm.1, f32[351,2,1024]{2,1,0:T(2,128)} %bitcast.2, bf16[2,512,768]{2,1,0:T(8,128)(2,1)} %constant.8.clone.forward_hbm, ...), custom_call_target="tpu_custom_call" | custom-call | tf_op jit(solution)/shard_map/pallas_call | solution.py:369
  32.0 2.3 %copy.12 = bf16[2048,256]{1,0:T(8,128)(2,1)} copy(bf16[2048,256]{1,0:T(8,128)(2,1)} %get-tuple-element.4) | data formatting | bytes 2097152
  34.2 2.3 %copy.13 = f32[1024,256]{1,0:T(8,128)} copy(f32[1024,256]{1,0:T(8,128)} %get-tuple-element.5) | data formatting | bytes 2097152

commit v5 on v4

--- a/solution.py
+++ b/solution.py
@@ -11,7 +11,8 @@
 LANES = 128
 TAP_GROUP = 128
 SUBLANES = 8
-CHUNK = 256
+CHUNK = 512
+COPIES = 4
 MESH = pl.DeviceIdType.MESH
 
 
@@ -366,7 +367,7 @@
     tiles = spectrum // (2 * LANES)
     chunks = rows // CHUNK
     hbm = pl.BlockSpec(memory_space=pl.ANY)
-    return pl.pallas_call(
+    results = pl.pallas_call(
         functools.partial(kernel, length, grid),
         out_shape=(
             jax.ShapeDtypeStruct((rows, share), jnp.bfloat16),
@@ -408,6 +409,27 @@
         strain, filters[0], synthesis, correlation.transpose(2, 1, 0),
         forward, series, inverse, band,
     )
+    return pl.pallas_call(
+        hand_over,
+        out_shape=tuple(jax.ShapeDtypeStruct(x.shape, x.dtype) for x in results),
+        in_specs=[hbm, hbm],
+        out_specs=(hbm, hbm),
+        scratch_shapes=[pltpu.SemaphoreType.DMA((2, COPIES))],
+        compiler_params=pltpu.CompilerParams(vmem_limit_bytes=56 * 2**20),
+    )(*results)
+
+
+def hand_over(snr_in, residual_in, snr_out, residual_out, sems):
+    copies = []
+    for k, (source, target) in enumerate([(snr_in, snr_out), (residual_in, residual_out)]):
+        part = source.shape[0] // COPIES
+        for i in range(COPIES):
+            at = pl.ds(i * part, part)
+            copies.append(pltpu.make_async_copy(source.at[at], target.at[at], sems.at[k, i]))
+    for copy in copies:
+        copy.start()
+    for copy in copies:
+        copy.wait()
 
 
 def solution(mesh):

time: 36.7 us -> 95.4 us (2.60)
  Pallas kernels: 31.3 us -> 94.6 us
  local copies, waits for them, and re-layouts: 4.52 us -> 0 us
    pallas_call x0 -> x1, Pallas kernels: none -> 64.7 us  [local(): pl.pallas_call(hand_over, out_shape=tuple((jax.ShapeDtypeStruct(x.shape,...]
    unnamed x2 -> x0, local copies, waits for them, and re-layouts: 4.52 us -> none
    pallas_call x1, Pallas kernels: 31.3 us -> 29.9 us  [local(): pl.pallas_call(functools.partial(kernel, length, grid), out_shape=(jax.Sh...]
where the time goes in v5:
time: 95.4 us; the launch traced here: 95.2 us
  Pallas kernels  94.6 us (99%)
    pallas_call x1, Pallas kernels, local(): pl.pallas_call(hand_over, out_shape=tuple((jax.ShapeDtypeStruct(x.shape,...  64.7 us
    pallas_call x1, Pallas kernels, local(): pl.pallas_call(functools.partial(kernel, length, grid), out_shape=(jax.Sh...  29.9 us

profile of v5, /device:TPU:0, one launch (start us, length us, event | category | flops | bytes accessed | tf_op | source)
XLA Modules:
  0.0 95.2 jit_solution(4039094850399794922)
XLA Ops:
  0.6 29.9 %shard_map.95 = (bf16[2048,256]{1,0:T(8,128)(2,1)}, f32[1024,256]{1,0:T(8,128)}) custom-call(bf16[1,1535]{1,0:T(2,128)(2,1)} %strain_hbm.1, bf16[64,1024]{1,0:T(8,128)(2,1)} %bitcast.3, bf16[1,2048,1024]{2,1,0:T(8,128)(2,1)} %synthesis_hbm.1, f32[351,2,1024]{2,1,0:T(2,128)} %bitcast.2, bf16[2,512,768]{2,1,0:T(8,128)(2,1)} %constant.8.clone.forward_hbm, ...), custom_call_target="tpu_custom_call" | custom-call | tf_op jit(solution)/shard_map/pallas_call | solution.py:370
  30.5 64.7 %shard_map.96 = (bf16[2048,256]{1,0:T(8,128)(2,1)}, f32[1024,256]{1,0:T(8,128)}) custom-call(bf16[2048,256]{1,0:T(8,128)(2,1)} %get-tuple-element.4.snr_in, f32[1024,256]{1,0:T(8,128)} %get-tuple-element.5.residual_in), custom_call_target="tpu_custom_call" | custom-call | tf_op jit(solution)/shard_map/pallas_call | solution.py:412

commit v6 on v5

--- a/solution.py
+++ b/solution.py
@@ -414,21 +414,28 @@
         out_shape=tuple(jax.ShapeDtypeStruct(x.shape, x.dtype) for x in results),
         in_specs=[hbm, hbm],
         out_specs=(hbm, hbm),
-        scratch_shapes=[pltpu.SemaphoreType.DMA((2, COPIES))],
+        scratch_shapes=[pltpu.VMEM(x.shape, x.dtype) for x in results]
+        + [pltpu.SemaphoreType.DMA((2, COPIES))] * 2,
         compiler_params=pltpu.CompilerParams(vmem_limit_bytes=56 * 2**20),
     )(*results)
 
 
-def hand_over(snr_in, residual_in, snr_out, residual_out, sems):
-    copies = []
-    for k, (source, target) in enumerate([(snr_in, snr_out), (residual_in, residual_out)]):
+def hand_over(snr_in, residual_in, snr_out, residual_out, snr, residual, into, out):
+    arrive, leave = [], []
+    for k, (source, held, target) in enumerate(
+        [(snr_in, snr, snr_out), (residual_in, residual, residual_out)]
+    ):
         part = source.shape[0] // COPIES
         for i in range(COPIES):
             at = pl.ds(i * part, part)
-            copies.append(pltpu.make_async_copy(source.at[at], target.at[at], sems.at[k, i]))
-    for copy in copies:
+            arrive.append(pltpu.make_async_copy(source.at[at], held.at[at], into.at[k, i]))
+            leave.append(pltpu.make_async_copy(held.at[at], target.at[at], out.at[k, i]))
+    for copy in arrive:
         copy.start()
-    for copy in copies:
+    for first, second in zip(arrive, leave):
+        first.wait()
+        second.start()
+    for copy in leave:
         copy.wait()
 
 

time: 95.4 us -> 33.1 us (0.35)
  Pallas kernels: 94.6 us -> 32.3 us
    pallas_call x1, Pallas kernels: 64.7 us -> 2.4 us  [local(): pl.pallas_call(hand_over, out_shape=tuple((jax.ShapeDtypeStruct(x.shape,...]
where the time goes in v6:
time: 33.1 us; the launch traced here: 32.9 us
  Pallas kernels  32.3 us (98%)
  between operations  0.64 us (2%)
    pallas_call x1, Pallas kernels, local(): pl.pallas_call(functools.partial(kernel, length, grid), out_shape=(jax.Sh...  29.9 us
    pallas_call x1, Pallas kernels, local(): pl.pallas_call(hand_over, out_shape=tuple((jax.ShapeDtypeStruct(x.shape,...  2.4 us

profile of v6, /device:TPU:0, one launch (start us, length us, event | category | flops | bytes accessed | tf_op | source)
XLA Modules:
  0.0 32.9 jit_solution(4254585897980680113)
XLA Ops:
  0.6 29.9 %shard_map.95 = (bf16[2048,256]{1,0:T(8,128)(2,1)}, f32[1024,256]{1,0:T(8,128)}) custom-call(bf16[1,1535]{1,0:T(2,128)(2,1)} %strain_hbm.1, bf16[64,1024]{1,0:T(8,128)(2,1)} %bitcast.3, bf16[1,2048,1024]{2,1,0:T(8,128)(2,1)} %synthesis_hbm.1, f32[351,2,1024]{2,1,0:T(2,128)} %bitcast.2, bf16[2,512,768]{2,1,0:T(8,128)(2,1)} %constant.8.clone.forward_hbm, ...), custom_call_target="tpu_custom_call" | custom-call | tf_op jit(solution)/shard_map/pallas_call | solution.py:370
  30.5 2.4 %shard_map.96 = (bf16[2048,256]{1,0:T(8,128)(2,1)}, f32[1024,256]{1,0:T(8,128)}) custom-call(bf16[2048,256]{1,0:T(8,128)(2,1)} %get-tuple-element.4.snr_in, f32[1024,256]{1,0:T(8,128)} %get-tuple-element.5.residual_in), custom_call_target="tpu_custom_call" | custom-call | tf_op jit(solution)/shard_map/pallas_call | solution.py:412
